TPU v7x, 512 devices: a whole 4x4x16 slice. The times are simulated.
512 devices in a mesh: dp: 16 (over x, z_hi, core), tm: 8 (over z_lo), height: 4 (over y).
Axes of the slice: x: 4, y: 4, z: 16 (z_hi: 2, z_lo: 8; z = z_hi * 8 + z_lo), core: 2. Of those that a mesh axis runs over, the one named last changes fastest.
Arguments:
- latent: bfloat16 [256, 8, 16, 512], P(('dp', 'tm'), None, None, 'height'), parts along dimension 0, may hold values from -6 to 6
- gain_latent: float32 [512], P('height'), may hold values from 0.25 to 1.75
- shift_latent: float32 [512], P('height'), may hold values from -3 to 3
- conv_latent: bfloat16 [13824, 512], P('tm', 'height'), may hold values from -0.0546875 to 0.0546875
- up_weight: bfloat16 [512, 2048], P('height'), may hold values from -0.25 to 0.25
- gain_block: float32 [256], replicated, may hold values from 0.25 to 1.75
- shift_block: float32 [256], replicated, may hold values from -3 to 3
- conv_block: bfloat16 [6912, 256], P(('tm', 'height')), may hold values from -0.078125 to 0.078125
- cotangent: bfloat16 [512, 16, 32, 256], P(('dp', 'tm'), 'height'), parts along dimension 0, may hold values from -6 to 6
Outputs:
- decoded: bfloat16 [512, 16, 32, 256], P(('dp', 'tm'), 'height'), parts along dimension 0
- grad_upsampled: bfloat16 [512, 16, 32, 256], P(('dp', 'tm'), 'height'), parts along dimension 0
- grad_weight: float32 [36864, 256], P(('dp', 'tm', 'height')), parts along dimension 0
- grad_gain: float32 [4096], P('dp'), parts along dimension 0
- grad_shift: float32 [4096], P('dp'), parts along dimension 0
There are 16 independent parts, one for each index of `dp`. A program takes and returns all parts, laid end to end along the dimension named above; an argument that names none is the same for every part. Nothing has to cross between parts.
All inputs are finite; a program needn't handle non-finite values.
Results may differ from a plain program's by a relative error of at most 0.009.
Values may be sent and summed in bfloat16 or wider, within the bound.
No kernel may reach another device: no remote copies, remote signals or barrier semaphores. Data moves between devices by JAX's collectives and lax.ppermute only.
A program may use at most 128 MiB of HBM per device.

v0:
```python
import jax
import jax.numpy as jnp
from jax import lax
from jax.sharding import PartitionSpec as P

C1 = 512
GROUPS = 32
epsilon = 1e-06


def copy_for_each(array, axis):
    devices = lax.axis_size(axis)
    return lax.all_to_all(
        jnp.broadcast_to(array[None], (devices, *array.shape)), axis, 0, 0, tiled=True
    )


def taken_together(array, axis):
    everything = copy_for_each(array, axis)
    return jnp.sum(everything, axis=0)


def packed_total(arrays, axis):
    ends = [0]
    for a in arrays:
        ends.append(ends[-1] + a.size)
    so_far = taken_together(jnp.concatenate([a.ravel() for a in arrays]), axis)
    return tuple((so_far[b:e].reshape(a.shape) for a, b, e in zip(arrays, ends, ends[1:])))


def shifted(block, axis, distance):
    devices = range(lax.axis_size(axis))
    route = [(i - distance, i) for i in devices if i - distance in devices]
    return lax.ppermute(block, axis, route)


def in_order(tiles, dim):
    tiles = jnp.moveaxis(tiles, 0, dim)
    shape = tiles.shape
    return tiles.reshape(*shape[:dim], shape[dim] * shape[dim + 1], *shape[dim + 2 :])


def gather_directly(array, axis, dim):
    tiles = copy_for_each(array, axis)
    return in_order(tiles, dim)


def extended_2(cells, sides, width):
    for axis, dim in sides:
        count = lax.axis_size(axis)
        ends = count - 1
        head = lax.slice_in_dim(cells, 0, width, axis=dim)
        tail = lax.slice_in_dim(cells, cells.shape[dim] - width, cells.shape[dim], axis=dim)
        cells = jnp.concatenate(
            [
                lax.ppermute(tail, axis, [(i, (i + 1) % count) for i in range(ends)]),
                cells,
                lax.ppermute(head, axis, [((i + 1) % count, i) for i in range(ends)]),
            ],
            axis=dim,
        )
    return cells


def gather_in_order(array, axes, turns):
    tiles = array
    for k in turns:
        tiles = lax.all_gather(tiles, axes[k])
    done = turns[::-1]
    back = [done.index(k) for k in range(len(axes))]
    tiles = tiles.transpose(*back, *range(len(axes), tiles.ndim))
    return tiles.reshape(-1, *array.shape)


def whole_of(array, axes, turns, dim):
    return in_order(gather_in_order(array, axes, turns), dim)


def cut_along(array, dim, devices):
    before, after = (array.shape[:dim], array.shape[dim + 1 :])
    return jnp.moveaxis(array.reshape(*before, devices, -1, *after), dim, 0)


def sum_at_owner(array, axis, dim):
    tiles = cut_along(array, dim, lax.axis_size(axis))
    arrived = lax.all_to_all(tiles, axis, split_axis=0, concat_axis=0, tiled=True)
    return arrived.sum(axis=0)


def standardize(values, mean_value, inverse, groups):
    shape_full = values.shape
    grouped = values.reshape(shape_full[:-1] + (groups, shape_full[-1] // groups))
    return ((grouped - mean_value[:, None]) * inverse[:, None]).reshape(shape_full)


def causal_taps(padded, weight, frames, rows, cols):
    channels_in = padded.shape[-1]
    summed = jnp.zeros((frames * rows * cols, weight.shape[1]), jnp.float32)
    for lag_step in range(3):
        for row_step in range(3):
            for col_step in range(3):
                tap_index = (lag_step * 3 + row_step) * 3 + col_step
                window = padded[
                    lag_step : lag_step + frames,
                    row_step : row_step + rows,
                    col_step : col_step + cols,
                ]
                kernel = weight[tap_index * channels_in : (tap_index + 1) * channels_in]
                summed = summed + jnp.dot(
                    window.reshape(-1, channels_in), kernel, preferred_element_type=jnp.float32
                )
    return summed.reshape(frames, rows, cols, weight.shape[1])


def transposed_taps(padded, weight, frames, rows, cols):
    channels_out = padded.shape[-1]
    channels_in = weight.shape[0] // 27
    summed = jnp.zeros((frames * rows * cols, channels_in), jnp.float32)
    for lag_step in range(3):
        for row_step in range(3):
            for col_step in range(3):
                tap_index = (lag_step * 3 + row_step) * 3 + col_step
                window = padded[
                    2 - lag_step : 2 - lag_step + frames,
                    2 - row_step : 2 - row_step + rows,
                    2 - col_step : 2 - col_step + cols,
                ]
                kernel = weight[tap_index * channels_in : (tap_index + 1) * channels_in]
                summed = summed + lax.dot_general(
                    window.reshape(-1, channels_out),
                    kernel,
                    (((1,), (1,)), ((), ())),
                    preferred_element_type=jnp.float32,
                )
    return summed.reshape(frames, rows, cols, channels_in)


def weight_terms(padded, grads, frames, rows, cols):
    channels_in = padded.shape[-1]
    flat_grads = grads.reshape(-1, grads.shape[-1])
    blocks = []
    for row_step in range(3):
        for col_step in range(3):
            window = padded[2 : 2 + frames, row_step : row_step + rows, col_step : col_step + cols]
            blocks.append(
                lax.dot_general(
                    window.reshape(-1, channels_in),
                    flat_grads,
                    (((0,), (0,)), ((), ())),
                    preferred_element_type=jnp.float32,
                )
            )
    return jnp.concatenate(blocks, 0)


def local(
    latent,
    gain_latent,
    shift_latent,
    conv_latent,
    up_weight,
    gain_block,
    shift_block,
    conv_block,
    cotangent,
):
    per_group = C1 // GROUPS
    groups_here = latent.shape[-1] // per_group
    latent_f32 = latent.astype(jnp.float32)
    grouped = latent_f32.reshape(-1, groups_here, per_group)
    first_sums = jnp.sum(grouped, axis=(0, 2))
    second_sums = jnp.sum(grouped * grouped, axis=(0, 2))
    first_totals, second_totals = packed_total((first_sums, second_sums), "tm")
    count_latent = grouped.shape[0] * per_group * lax.axis_size("tm")
    mean_latent = first_totals / count_latent
    inverse_latent = lax.rsqrt(second_totals / count_latent - mean_latent * mean_latent + epsilon)
    normed = (
        standardize(latent_f32, mean_latent, inverse_latent, groups_here) * gain_latent
        + shift_latent
    )
    active = jax.nn.silu(normed).astype(jnp.bfloat16)
    earlier = shifted(active, "tm", 1)
    extended = jnp.concatenate([earlier, active], 0)
    all_channels = gather_directly(extended, "height", 3)
    padded = jnp.pad(all_channels, ((0, 0), (1, 1), (1, 1), (0, 0)))
    latent_weight = lax.all_gather(conv_latent, "tm", axis=0, tiled=True)
    frames_latent, rows_latent, cols_latent = (latent.shape[0], latent.shape[1], latent.shape[2])
    mixed = causal_taps(padded, latent_weight, frames_latent, rows_latent, cols_latent)
    refined = (latent_f32 + mixed).astype(jnp.bfloat16)
    band_rows = rows_latent // lax.axis_size("height")
    own_band = lax.all_to_all(refined, "height", split_axis=1, concat_axis=3, tiled=True)
    flat_band = own_band.reshape(-1, own_band.shape[-1])
    expanded = jnp.dot(
        flat_band, gather_directly(up_weight, "height", 0), preferred_element_type=jnp.float32
    )
    channels_block = up_weight.shape[1] // 8
    spread = expanded.reshape(frames_latent, band_rows, cols_latent, 2, 2, 2, channels_block)
    spread = spread.transpose(0, 3, 1, 4, 2, 5, 6)
    upsampled = spread.reshape(
        2 * frames_latent, 2 * band_rows, 2 * cols_latent, channels_block
    ).astype(jnp.bfloat16)
    frames_block, rows_block, cols_block = (
        upsampled.shape[0],
        upsampled.shape[1],
        upsampled.shape[2],
    )
    up_f32 = upsampled.astype(jnp.float32)
    per_block = channels_block // GROUPS
    grouped_block = up_f32.reshape(-1, GROUPS, per_block)
    block_first = jnp.sum(grouped_block, axis=(0, 2))
    block_second = jnp.sum(grouped_block * grouped_block, axis=(0, 2))
    block_first, block_second = packed_total((block_first, block_second), ("tm", "height"))
    count_block = grouped_block.shape[0] * per_block * lax.axis_size("tm") * lax.axis_size("height")
    mean_block = block_first / count_block
    inverse_block = lax.rsqrt(block_second / count_block - mean_block * mean_block + epsilon)
    standard = standardize(up_f32, mean_block, inverse_block, GROUPS)
    normed_block = standard * gain_block + shift_block
    active_block = jax.nn.silu(normed_block).astype(jnp.bfloat16)
    before = shifted(active_block[-2:], "tm", 1)
    ext_block = jnp.concatenate([before, active_block], 0)
    beside_all = extended_2(ext_block, (("height", 1),), 1)
    padded_block = jnp.pad(beside_all, ((0, 0), (0, 0), (1, 1), (0, 0)))
    block_weight = whole_of(conv_block, ("tm", "height"), (0, 1), 0)
    mixed_block = causal_taps(padded_block, block_weight, frames_block, rows_block, cols_block)
    decoded = (up_f32 + mixed_block).astype(jnp.bfloat16)
    after = shifted(cotangent[:2], "tm", -1)
    grad_ext = jnp.concatenate([cotangent, after], 0)
    grad_around = extended_2(grad_ext, (("height", 1),), 1)
    grad_padded = jnp.pad(grad_around, ((0, 0), (0, 0), (1, 1), (0, 0)))
    grad_active = transposed_taps(grad_padded, block_weight, frames_block, rows_block, cols_block)
    local_terms = weight_terms(padded_block, cotangent, frames_block, rows_block, cols_block)
    time_summed = sum_at_owner(local_terms, "tm", 0)
    grad_weight = sum_at_owner(time_summed, "height", 0)
    sigmoid = jax.nn.sigmoid(normed_block)
    grad_normed = grad_active * sigmoid * (1.0 + normed_block * (1.0 - sigmoid))
    flat_grad = grad_normed.reshape(-1, channels_block)
    flat_standard = standard.reshape(-1, channels_block)
    grad_shift, grad_gain = packed_total(
        (jnp.sum(flat_grad, axis=0), jnp.sum(flat_grad * flat_standard, axis=0)), ("tm", "height")
    )
    first_mean = jnp.sum((gain_block * grad_shift).reshape(GROUPS, per_block), axis=1) / count_block
    second_mean = jnp.sum((gain_block * grad_gain).reshape(GROUPS, per_block), axis=1) / count_block
    grouped_grad = (grad_normed * gain_block).reshape(-1, GROUPS, per_block)
    grouped_standard = standard.reshape(-1, GROUPS, per_block)
    corrected = (
        grouped_grad - first_mean[:, None] - grouped_standard * second_mean[:, None]
    ) * inverse_block[:, None]
    grad_upsampled = (cotangent.astype(jnp.float32) + corrected.reshape(cotangent.shape)).astype(
        jnp.bfloat16
    )
    return (decoded, grad_upsampled, grad_weight, grad_gain, grad_shift)


def solution(mesh):
    return jax.shard_map(
        local,
        mesh=mesh,
        in_specs=(
            P(("dp", "tm"), None, None, "height"),
            P("height"),
            P("height"),
            P("tm", "height"),
            P("height", None),
            P(),
            P(),
            P(("tm", "height"), None),
            P(("dp", "tm"), "height", None, None),
        ),
        out_specs=(
            P(("dp", "tm"), "height", None, None),
            P(("dp", "tm"), "height", None, None),
            P(("dp", "tm", "height"), None),
            P("dp"),
            P("dp"),
        ),
        check_vma=False,
    )
```

profile of v0, /device:TPU:2, one launch (start us, length us, event | category | flops | bytes accessed | tf_op | source)
XLA Modules:
  0.0 456.5 jit_solution(3244054950084139941)
XLA Ops:
  7.2 54.2 %all-gather = bf16[1728,256]{1,0:T(8,128)(2,1)} all-gather(bf16[216,256]{1,0:T(8,128)(2,1)} %param.16), channel_id=2, replica_groups=mesh['dp'=16,'tm'=8,'height'=4] {'tm'}, dimensions={0}, use_global_device_ids=true | all-gather | bytes 995328 | tf_op jit(solution)/shard_map/all_gather | solution.py:68
  63.4 10.3 %all-to-all-start = ((f32[8,1,16]{2,1,0:T(1,128)}), f32[8,1,16]{2,1,0:T(1,128)S(1)}, u32[]{:S(2)}, u32[]{:S(2)}) async-start(f32[8,1,16]{2,1,0:T(1,128)} %broadcast_in_dim.10), calls=%async_computation | async-start | bytes 8192 | tf_op jit(solution)/shard_map/all_to_all | solution.py:13
  73.7 0.9 slice.629
  74.6 1.3 collective-permute-start.4
  75.9 8.1 %all-to-all-done = f32[8,1,16]{2,1,0:T(1,128)S(1)} async-done(((f32[8,1,16]{2,1,0:T(1,128)}), f32[8,1,16]{2,1,0:T(1,128)S(1)}, u32[]{:S(2)}, u32[]{:S(2)}) %all-to-all-start) | async-done | bytes 544 | tf_op jit(solution)/shard_map/all_to_all | solution.py:13
  84.4 0.9 fusion.44
  85.3 2.5 collective-permute-start
  87.8 1.0 constant_dynamic-update-slice_fusion.1
  88.8 0.9 collective-permute-done
  89.8 0.9 broadcast_in_dim.11
  90.7 4.5 all-to-all-start.1
  95.2 1.3 collective-permute-start.6
  96.5 4.6 collective-permute-start.5
  101.4 8.3 %all-to-all-done.1 = bf16[4,4,8,16,128]{4,3,2,1,0:T(8,128)(2,1)S(1)} async-done(((bf16[4,4,8,16,128]{4,3,2,1,0:T(8,128)(2,1)}), bf16[4,4,8,16,128]{4,3,2,1,0:T(8,128)(2,1)S(1)}, u32[]{:S(2)}, u32[]{:S(2)}) %all-to-all-start.1) | async-done | bytes 524320 | tf_op jit(solution)/shard_map/all_to_all | solution.py:13
  109.6 1.7 broadcast_in_dim.12
  111.3 3.6 all-to-all-start.3
  115.3 1.4 pad_maximum_fusion.1
  116.7 2.2 fusion.149
  119.1 0.9 copy.69
  121.9 1.2 pad_slice_fusion.1
  123.1 2.4 pad_slice_fusion
  125.4 19.1 %all-to-all-done.3 = bf16[4,128,2048]{1,2,0:T(8,128)(2,1)S(1)} async-done(((bf16[4,128,2048]{1,2,0:T(8,128)(2,1)}), bf16[4,128,2048]{1,2,0:T(8,128)(2,1)S(1)}, u32[]{:S(2)}, u32[]{:S(2)}) %all-to-all-start.3) | async-done | bytes 2097184 | tf_op jit(solution)/shard_map/all_to_all | solution.py:13
  144.5 2.6 copy.75
  147.2 3.9 copy.76
  151.1 2.4 copy.79
  160.1 1.1 convolution_add_fusion.2
  161.2 68.7 %all-gather.5.cloned.1.call-done = bf16[13824,128]{1,0:T(8,128)(2,1)} async-done(((bf16[1728,128]{1,0:T(8,128)(2,1)}), bf16[13824,128]{1,0:T(8,128)(2,1)}) %all-gather.5.cloned.1.call-update) | async-done | bytes 3538960 | tf_op jit(solution)/shard_map/all_gather | solution.py:186
  229.9 1.3 fusion.72
  231.3 1.4 convolution_add_fusion.72
  232.6 1.2 convolution_add_fusion.71
  233.9 1.2 convolution_add_fusion.70
  235.1 1.2 convolution_add_fusion.69
  236.4 1.2 convolution_add_fusion.68
  237.7 1.2 convolution_add_fusion.67
  238.9 1.2 convolution_add_fusion.66
  245.2 4.2 all-to-all-start.2
  249.4 2.2 convolution_add_fusion.1
  251.6 3.6 all-to-all-done.2
  255.2 1.5 copy.119
  256.7 1.5 reshape.488
  258.2 3.7 fusion.146
  266.1 4.8 %all-to-all-start.4 = ((f32[32,1,64]{2,1,0:T(1,128)}), f32[32,1,64]{2,1,0:T(1,128)S(1)}, u32[]{:S(2)}, u32[]{:S(2)}) async-start(f32[32,1,64]{2,1,0:T(1,128)} %broadcast_in_dim.13), calls=%async_computation.4 | async-start | bytes 32768 | tf_op jit(solution)/shard_map/all_to_all | solution.py:13
  270.9 2.0 fusion.74
  272.9 2.2 copy.77
  275.2 2.2 reshape.485
  277.4 5.9 %all-to-all-done.4 = f32[32,1,64]{2,1,0:T(1,128)S(1)} async-done(((f32[32,1,64]{2,1,0:T(1,128)}), f32[32,1,64]{2,1,0:T(1,128)S(1)}, u32[]{:S(2)}, u32[]{:S(2)}) %all-to-all-start.4) | async-done | bytes 8224 | tf_op jit(solution)/shard_map/all_to_all | solution.py:13
  283.8 1.2 slice_multiply_fusion
  287.1 2.8 fusion.145
  290.6 6.5 %all-to-all-start.5 = ((f32[32,1,512]{2,1,0:T(1,128)}), f32[32,1,512]{2,1,0:T(1,128)S(1)}, u32[]{:S(2)}, u32[]{:S(2)}) async-start(f32[32,1,512]{2,1,0:T(1,128)} %broadcast_in_dim.14), calls=%async_computation.5 | async-start | bytes 131072 | tf_op jit(solution)/shard_map/all_to_all | solution.py:13
  297.1 1.4 reshape.484
  298.5 11.5 %all-to-all-done.5 = f32[32,1,512]{2,1,0:T(1,128)S(1)} async-done(((f32[32,1,512]{2,1,0:T(1,128)}), f32[32,1,512]{2,1,0:T(1,128)S(1)}, u32[]{:S(2)}, u32[]{:S(2)}) %all-to-all-start.5) | async-done | bytes 65568 | tf_op jit(solution)/shard_map/all_to_all | solution.py:13
  311.4 2.2 add_convert_fusion
  313.6 2.3 collective-permute-start.1
  315.9 2.5 collective-permute-done.1
  318.5 1.3 collective-permute-start.3
  319.8 4.6 collective-permute-start.2
  325.0 1.5 collective-permute-done.2
  329.4 1.4 copy-done.9
  330.8 5.2 %all-to-all-start.6 = ((f32[8,288,256]{2,1,0:T(8,128)}), f32[8,288,256]{2,1,0:T(8,128)S(1)}, u32[]{:S(2)}, u32[]{:S(2)}) async-start(f32[8,288,256]{2,1,0:T(8,128)} %bitcast.329), calls=%async_computation.6 | async-start | bytes 4718592 | tf_op jit(solution)/shard_map/all_to_all | solution.py:86
  336.1 1.0 pad_maximum_fusion
  337.9 1.3 copy-done.1
  345.7 91.6 %all-to-all-done.6 = f32[8,288,256]{2,1,0:T(8,128)S(1)} async-done(((f32[8,288,256]{2,1,0:T(8,128)}), f32[8,288,256]{2,1,0:T(8,128)S(1)}, u32[]{:S(2)}, u32[]{:S(2)}) %all-to-all-start.6) | async-done | bytes 2359328 | tf_op jit(solution)/shard_map/all_to_all | solution.py:86
  438.2 4.0 all-to-all-start.7
  443.0 6.1 %all-to-all-done.7 = f32[4,72,256]{2,1,0:T(8,128)S(1)} async-done(((f32[4,72,256]{2,1,0:T(8,128)}), f32[4,72,256]{2,1,0:T(8,128)S(1)}, u32[]{:S(2)}, u32[]{:S(2)}) %all-to-all-start.7) | async-done | bytes 294944 | tf_op jit(solution)/shard_map/all_to_all | solution.py:86
  (265 shorter events, 38.0 us)
Async XLA Ops:
  7.2 93.9 %copy-start.53 = (bf16[128,2048]{1,0:T(8,128)(2,1)S(1)}, bf16[128,2048]{1,0:T(8,128)(2,1)}, u32[]{:S(2)}) copy-start(bf16[128,2048]{1,0:T(8,128)(2,1)} %param.13) | copy-start | bytes 1572868
  7.2 143.9 %all-gather.7.cloned.1.call-start = ((), (), s32[]{:S(2)}) async-start(), calls=%async_computation.9 | async-start | bytes 4423680 | tf_op jit(solution)/shard_map/all_gather | solution.py:68
  63.4 20.6 %all-to-all-start = ((f32[8,1,16]{2,1,0:T(1,128)}), f32[8,1,16]{2,1,0:T(1,128)S(1)}, u32[]{:S(2)}, u32[]{:S(2)}) async-start(f32[8,1,16]{2,1,0:T(1,128)} %broadcast_in_dim.10), calls=%async_computation | async-start | bytes 8192 | tf_op jit(solution)/shard_map/all_to_all | solution.py:13
  74.6 20.5 %collective-permute-start.4 = (bf16[2,4,32,256]{3,2,1,0:T(8,128)(2,1)S(1)}, bf16[2,4,32,256]{3,2,1,0:T(8,128)(2,1)S(1)}, u32[]{:S(2)}, u32[]{:S(2)}) collective-permute-start(bf16[2,4,32,256]{3,2,1,0:T(8,128)(2,1)S(1)} %slice.629), channel_id=1, source_target_pairs={{4,0},{8,4},{12,8},{16,12},{20,16},{24,20},{28,24},{5,1},{9,5},{13... | collective-permute-start | bytes 393224 | tf_op jit(solution)/shard_map/ppermute | solution.py:34
  85.3 4.4 collective-permute-start
  90.7 18.9 %all-to-all-start.1 = ((bf16[4,4,8,16,128]{4,3,2,1,0:T(8,128)(2,1)}), bf16[4,4,8,16,128]{4,3,2,1,0:T(8,128)(2,1)S(1)}, u32[]{:S(2)}, u32[]{:S(2)}) async-start(bf16[4,4,8,16,128]{4,3,2,1,0:T(8,128)(2,1)} %broadcast_in_dim.11), calls=%async_computation.1 | async-start | bytes 1048576 | tf_op jit(solution)/shard_map/all_to_all | solution.py:13
  95.1 134.7 %all-gather.5.cloned.1.call-start = ((), (), s32[]{:S(2)}) async-start(), calls=%async_computation.8 | async-start | bytes 3981312 | tf_op jit(solution)/shard_map/all_gather | solution.py:186
  95.2 19.7 %collective-permute-start.6 = (bf16[6,1,32,256]{3,2,1,0:T(8,128)(2,1)S(1)}, bf16[6,1,32,256]{3,2,1,0:T(8,128)(2,1)S(1)}, u32[]{:S(2)}, u32[]{:S(2)}) collective-permute-start(bf16[6,1,32,256]{3,2,1,0:T(8,128)(2,1)S(1)} %get-tuple-element.98), channel_id=1, source_target_pairs={{1,0},{2,1},{3,2},{5,4},{6,5},{7,6},{9,8},{10,9},{11,10},{13,12},{... | collective-permute-start | bytes 294920 | tf_op jit(solution)/shard_map/ppermute | solution.py:58
  96.5 18.4 %collective-permute-start.5 = (bf16[6,1,32,256]{3,2,1,0:T(8,128)(2,1)S(1)}, bf16[6,1,32,256]{3,2,1,0:T(8,128)(2,1)S(1)}, u32[]{:S(2)}, u32[]{:S(2)}) collective-permute-start(bf16[6,1,32,256]{3,2,1,0:T(8,128)(2,1)S(1)} %get-tuple-element.97), channel_id=1, source_target_pairs={{0,1},{1,2},{2,3},{4,5},{5,6},{6,7},{8,9},{9,10},{10,11},{12,13},{... | collective-permute-start | bytes 294920 | tf_op jit(solution)/shard_map/ppermute | solution.py:56
  109.6 1.7 copy-start.2
  111.3 33.2 %all-to-all-start.3 = ((bf16[4,128,2048]{1,2,0:T(8,128)(2,1)}), bf16[4,128,2048]{1,2,0:T(8,128)(2,1)S(1)}, u32[]{:S(2)}, u32[]{:S(2)}) async-start(bf16[4,128,2048]{1,2,0:T(8,128)(2,1)} %broadcast_in_dim.12), calls=%async_computation.3 | async-start | bytes 4194304 | tf_op jit(solution)/shard_map/all_to_all | solution.py:13
  116.7 2.2 copy-start.3
  151.1 2.4 copy-start.16
  151.1 2.7 copy-start.15
  151.1 3.0 copy-start.14
  151.1 3.3 copy-start.13
  153.5 133.6 %copy-start = (bf16[8,4,216,256]{3,2,1,0:T(8,128)(2,1)}, bf16[8,4,216,256]{3,2,1,0:T(8,128)(2,1)S(1)}, u32[]{:S(2)}) copy-start(bf16[8,4,216,256]{3,2,1,0:T(8,128)(2,1)S(1)} %copy.79) | copy-start | bytes 10616836
  153.5 1.7 copy-start.37
  153.8 1.7 copy-start.12
  154.4 1.5 copy-start.36
  154.7 1.4 copy-start.30
  155.0 1.4 copy-start.35
  155.3 1.4 copy-start.33
  157.0 1.4 copy-start.23
  157.3 1.4 copy-start.28
  157.5 1.4 copy-start.27
  229.9 7.8 %copy-start.6 = (bf16[13824,128]{1,0:T(8,128)(2,1)S(1)}, bf16[13824,128]{1,0:T(8,128)(2,1)}, u32[]{:S(2)}) copy-start(bf16[13824,128]{1,0:T(8,128)(2,1)} %all-gather.5.cloned.1.call-done) | copy-start | bytes 10616836
  229.9 10.2 %copy-start.51 = (bf16[2,8,16,512]{3,2,1,0:T(8,128)(2,1)S(1)}, bf16[2,8,16,512]{3,2,1,0:T(8,128)(2,1)}, u32[]{:S(2)}) copy-start(bf16[2,8,16,512]{3,2,1,0:T(8,128)(2,1)} %get-tuple-element.60) | copy-start | bytes 786436
  229.9 10.4 %copy-start.50 = (bf16[2,8,16,512]{3,2,1,0:T(8,128)(2,1)S(1)}, bf16[2,8,16,512]{3,2,1,0:T(8,128)(2,1)}, u32[]{:S(2)}) copy-start(bf16[2,8,16,512]{3,2,1,0:T(8,128)(2,1)} %get-tuple-element.61) | copy-start | bytes 786436
  229.9 10.7 %copy-start.49 = (bf16[2,8,16,512]{3,2,1,0:T(8,128)(2,1)S(1)}, bf16[2,8,16,512]{3,2,1,0:T(8,128)(2,1)}, u32[]{:S(2)}) copy-start(bf16[2,8,16,512]{3,2,1,0:T(8,128)(2,1)} %get-tuple-element.62) | copy-start | bytes 786436
  229.9 10.9 %copy-start.48 = (bf16[2,8,16,512]{3,2,1,0:T(8,128)(2,1)S(1)}, bf16[2,8,16,512]{3,2,1,0:T(8,128)(2,1)}, u32[]{:S(2)}) copy-start(bf16[2,8,16,512]{3,2,1,0:T(8,128)(2,1)} %get-tuple-element.63) | copy-start | bytes 786436
  231.2 9.8 %copy-start.47 = (bf16[2,8,16,512]{3,2,1,0:T(8,128)(2,1)S(1)}, bf16[2,8,16,512]{3,2,1,0:T(8,128)(2,1)}, u32[]{:S(2)}) copy-start(bf16[2,8,16,512]{3,2,1,0:T(8,128)(2,1)} %get-tuple-element.64) | copy-start | bytes 786436
  232.6 8.7 %copy-start.22 = (bf16[2,8,16,4,128]{4,3,2,1,0:T(4,128)(2,1)S(1)}, bf16[2,8,16,4,128]{4,3,2,1,0:T(4,128)(2,1)}, u32[]{:S(2)}) copy-start(bf16[2,8,16,4,128]{4,3,2,1,0:T(4,128)(2,1)} %copy.70) | copy-start | bytes 786436
  233.9 7.7 %copy-start.46 = (bf16[2,8,16,512]{3,2,1,0:T(8,128)(2,1)S(1)}, bf16[2,8,16,512]{3,2,1,0:T(8,128)(2,1)}, u32[]{:S(2)}) copy-start(bf16[2,8,16,512]{3,2,1,0:T(8,128)(2,1)} %get-tuple-element.65) | copy-start | bytes 786436
  235.1 6.6 %copy-start.45 = (bf16[2,8,16,512]{3,2,1,0:T(8,128)(2,1)S(1)}, bf16[2,8,16,512]{3,2,1,0:T(8,128)(2,1)}, u32[]{:S(2)}) copy-start(bf16[2,8,16,512]{3,2,1,0:T(8,128)(2,1)} %get-tuple-element.66) | copy-start | bytes 786436
  236.4 5.6 %copy-start.44 = (bf16[2,8,16,512]{3,2,1,0:T(8,128)(2,1)S(1)}, bf16[2,8,16,512]{3,2,1,0:T(8,128)(2,1)}, u32[]{:S(2)}) copy-start(bf16[2,8,16,512]{3,2,1,0:T(8,128)(2,1)} %get-tuple-element.67) | copy-start | bytes 786436
  237.6 4.6 %copy-start.43 = (bf16[2,8,16,512]{3,2,1,0:T(8,128)(2,1)S(1)}, bf16[2,8,16,512]{3,2,1,0:T(8,128)(2,1)}, u32[]{:S(2)}) copy-start(bf16[2,8,16,512]{3,2,1,0:T(8,128)(2,1)} %get-tuple-element.68) | copy-start | bytes 786436
  238.9 3.6 copy-start.42
  240.1 2.6 copy-start.41
  240.3 2.6 copy-start.40
  240.6 2.6 copy-start.20
  240.8 2.6 copy-start.21
  241.1 2.6 copy-start.19
  241.3 2.6 copy-start.18
  241.5 2.5 copy-start.17
  241.8 2.5 copy-start.39
  242.0 2.5 copy-start.52
  245.2 10.0 %all-to-all-start.2 = ((bf16[2,8,16,128]{3,2,0,1:T(8,128)(2,1)}), bf16[2,8,16,128]{3,2,0,1:T(8,128)(2,1)}, u32[]{:S(2)}, u32[]{:S(2)}) async-start(bf16[2,8,16,128]{3,2,0,1:T(8,128)(2,1)} %fusion.45), calls=%async_computation.2 | async-start | bytes 131072 | tf_op jit(solution)/shard_map/all_to_all | solution.py:191
  266.1 17.1 %all-to-all-start.4 = ((f32[32,1,64]{2,1,0:T(1,128)}), f32[32,1,64]{2,1,0:T(1,128)S(1)}, u32[]{:S(2)}, u32[]{:S(2)}) async-start(f32[32,1,64]{2,1,0:T(1,128)} %broadcast_in_dim.13), calls=%async_computation.4 | async-start | bytes 32768 | tf_op jit(solution)/shard_map/all_to_all | solution.py:13
  287.1 22.9 %copy-start.57 = (f32[256]{0:T(256)S(1)}, f32[256]{0:T(256)}, u32[]{:S(2)}) copy-start(f32[256]{0:T(256)} %param.14) | copy-start | bytes 3076
  287.1 24.3 %copy-start.58 = (f32[256]{0:T(256)S(1)}, f32[256]{0:T(256)}, u32[]{:S(2)}) copy-start(f32[256]{0:T(256)} %mul.160) | copy-start | bytes 3076
  287.1 24.3 %copy-start.59 = (f32[256]{0:T(256)S(1)}, f32[256]{0:T(256)}, u32[]{:S(2)}) copy-start(f32[256]{0:T(256)} %sub.74) | copy-start | bytes 3076
  287.1 24.3 %copy-start.60 = (f32[256]{0:T(256)S(1)}, f32[256]{0:T(256)}, u32[]{:S(2)}) copy-start(f32[256]{0:T(256)} %param.15) | copy-start | bytes 3076
  289.9 37.0 %copy-start.8 = (bf16[4,4,32,256]{3,2,1,0:T(8,128)(2,1)S(1)}, bf16[4,4,32,256]{3,2,1,0:T(8,128)(2,1)}, u32[]{:S(2)}) copy-start(bf16[4,4,32,256]{3,2,1,0:T(8,128)(2,1)} %param.17) | copy-start | bytes 786436
  290.6 19.4 %all-to-all-start.5 = ((f32[32,1,512]{2,1,0:T(1,128)}), f32[32,1,512]{2,1,0:T(1,128)S(1)}, u32[]{:S(2)}, u32[]{:S(2)}) async-start(f32[32,1,512]{2,1,0:T(1,128)} %broadcast_in_dim.14), calls=%async_computation.5 | async-start | bytes 131072 | tf_op jit(solution)/shard_map/all_to_all | solution.py:13
  298.5 26.5 %copy-start.4 = (f32[4,4,32,256]{3,2,1,0:T(8,128)}, f32[4,4,32,256]{3,2,1,0:T(8,128)S(1)}, u32[]{:S(2)}) copy-start(f32[4,4,32,256]{3,2,1,0:T(8,128)S(1)} %reshape.484) | copy-start | bytes 1572868
  313.6 4.8 %collective-permute-start.1 = (bf16[2,4,32,256]{3,2,1,0:T(8,128)(2,1)S(1)}, bf16[2,4,32,256]{3,2,1,0:T(8,128)(2,1)S(1)}, u32[]{:S(2)}, u32[]{:S(2)}) collective-permute-start(bf16[2,4,32,256]{3,2,1,0:T(8,128)(2,1)S(1)} %slice.690), channel_id=1, source_target_pairs={{0,4},{4,8},{8,12},{12,16},{16,20},{20,24},{24,28},{1,5},{5,9},{9,... | collective-permute-start | bytes 393224 | tf_op jit(solution)/shard_map/ppermute | solution.py:34
  318.5 6.5 %collective-permute-start.3 = (bf16[6,1,32,256]{3,2,1,0:T(8,128)(2,1)S(1)}, bf16[6,1,32,256]{3,2,1,0:T(8,128)(2,1)S(1)}, u32[]{:S(2)}, u32[]{:S(2)}) collective-permute-start(bf16[6,1,32,256]{3,2,1,0:T(8,128)(2,1)S(1)} %get-tuple-element.104), channel_id=1, source_target_pairs={{1,0},{2,1},{3,2},{5,4},{6,5},{7,6},{9,8},{10,9},{11,10},{13,12},{... | collective-permute-start | bytes 294920 | tf_op jit(solution)/shard_map/ppermute | solution.py:58
  319.8 6.8 %collective-permute-start.2 = (bf16[6,1,32,256]{3,2,1,0:T(8,128)(2,1)S(1)}, bf16[6,1,32,256]{3,2,1,0:T(8,128)(2,1)S(1)}, u32[]{:S(2)}, u32[]{:S(2)}) collective-permute-start(bf16[6,1,32,256]{3,2,1,0:T(8,128)(2,1)S(1)} %get-tuple-element.103), channel_id=1, source_target_pairs={{0,1},{1,2},{2,3},{4,5},{5,6},{6,7},{8,9},{9,10},{10,11},{12,13},{... | collective-permute-start | bytes 294920 | tf_op jit(solution)/shard_map/ppermute | solution.py:56
  325.0 3.9 copy-start.55
  330.8 106.5 %all-to-all-start.6 = ((f32[8,288,256]{2,1,0:T(8,128)}), f32[8,288,256]{2,1,0:T(8,128)S(1)}, u32[]{:S(2)}, u32[]{:S(2)}) async-start(f32[8,288,256]{2,1,0:T(8,128)} %bitcast.329), calls=%async_computation.6 | async-start | bytes 4718592 | tf_op jit(solution)/shard_map/all_to_all | solution.py:86
  337.1 2.0 copy-start.1
  345.0 97.2 %copy-start.5 = (f32[4,4,32,256]{3,2,1,0:T(8,128)S(1)}, f32[4,4,32,256]{3,2,1,0:T(8,128)}, u32[]{:S(2)}) copy-start(f32[4,4,32,256]{3,2,1,0:T(8,128)} %copy-done.4) | copy-start | bytes 1572868
  438.2 10.8 %all-to-all-start.7 = ((f32[4,72,256]{2,1,0:T(8,128)}), f32[4,72,256]{2,1,0:T(8,128)S(1)}, u32[]{:S(2)}, u32[]{:S(2)}) async-start(f32[4,72,256]{2,1,0:T(8,128)} %bitcast.332), calls=%async_computation.7 | async-start | bytes 589824 | tf_op jit(solution)/shard_map/all_to_all | solution.py:86
  (14 other events, 19.1 us)
Sparse Core Ops, SparseCore 0:
  61.5 69.8 all-gather.6
  133.5 96.3 all-gather.4
where the time goes:
time: 458 us; the launch traced here: 457 us
  waiting for transfers between devices  228 us (50%)
  starting transfers between devices  60.9 us (13%)
  blocking collectives  54.2 us (12%)
  local copies, waits for them, and re-layouts  41.6 us (9%)
  matrix products  40.5 us (9%)
  between operations  15.6 us (3%)
  other arithmetic  15.3 us (3%)
    all_to_all x2, waiting for transfers between devices, sum_at_owner(): lax.all_to_all(tiles, axis, split_axis=0, concat_axis=0, tiled=True)  97.7 us
    all_gather x1, waiting for transfers between devices, local(): latent_weight = lax.all_gather(conv_latent, 'tm', axis=0, tiled=True)  68.7 us
    all_gather x1, blocking collectives, gather_in_order(): tiles = lax.all_gather(tiles, axes[k])  54.2 us
    all_to_all x5, waiting for transfers between devices, copy_for_each(): lax.all_to_all(jnp.broadcast_to(array[None], (devices, *array.shape)), ax...  52.8 us
    all_to_all x5, starting transfers between devices, copy_for_each(): lax.all_to_all(jnp.broadcast_to(array[None], (devices, *array.shape)), ax...  29.7 us
    dot_general x54, matrix products, causal_taps(): jnp.dot(window.reshape(-1, channels_in), kernel, preferred_element_type=j...  20.3 us
    dot_general x27, matrix products, transposed_taps(): lax.dot_general(window.reshape(-1, channels_out), kernel, (((1,), (1,)),...  14 us
    all_to_all x2, starting transfers between devices, sum_at_owner(): lax.all_to_all(tiles, axis, split_axis=0, concat_axis=0, tiled=True)  9.22 us
  transfers between devices with their start and end apart: 17, of which 13 were waited for; matrix products, arithmetic and copies ran while one was open for 12% of the time, Pallas kernels for 0%

commit v1 on v0

--- a/solution.py
+++ b/solution.py
@@ -183,7 +183,9 @@
     extended = jnp.concatenate([earlier, active], 0)
     all_channels = gather_directly(extended, "height", 3)
     padded = jnp.pad(all_channels, ((0, 0), (1, 1), (1, 1), (0, 0)))
-    latent_weight = lax.all_gather(conv_latent, "tm", axis=0, tiled=True)
+    latent_weight = jnp.concatenate(
+        lax.all_to_all(jnp.stack([conv_latent] * lax.axis_size("tm")), "tm", 0, 0), axis=0
+    )
     frames_latent, rows_latent, cols_latent = (latent.shape[0], latent.shape[1], latent.shape[2])
     mixed = causal_taps(padded, latent_weight, frames_latent, rows_latent, cols_latent)
     refined = (latent_f32 + mixed).astype(jnp.bfloat16)

time: 458 us -> 580 us (1.27)
  blocking collectives: 54.2 us -> 235 us
  waiting for transfers between devices: 228 us -> 154 us
  matrix products: 40.5 us -> 57.8 us
    all_gather x1, blocking collectives: 54.2 us -> 187 us  [gather_in_order(): tiles = lax.all_gather(tiles, axes[k])]
    all_gather x1 -> x0, waiting for transfers between devices: 68.7 us -> none  [local(): latent_weight = lax.all_gather(conv_latent, 'tm', axis=0, tiled=True)]
    all_to_all x0 -> x2, blocking collectives: none -> 48.1 us  [copy_for_each(): lax.all_to_all(jnp.broadcast_to(array[None], (devices, *array.shape)), ax...]
    all_to_all x5 -> x3, waiting for transfers between devices: 52.8 us -> 24 us  [copy_for_each(): lax.all_to_all(jnp.broadcast_to(array[None], (devices, *array.shape)), ax...]
    dot_general x54, matrix products: 20.3 us -> 37.6 us  [causal_taps(): jnp.dot(window.reshape(-1, channels_in), kernel, preferred_element_type=j...]
    all_gather x1, waiting for transfers between devices: 0.01 us -> 11.6 us  [gather_in_order(): tiles = lax.all_gather(tiles, axes[k])]
    all_to_all x5 -> x3, starting transfers between devices: 29.7 us -> 22.2 us  [copy_for_each(): lax.all_to_all(jnp.broadcast_to(array[None], (devices, *array.shape)), ax...]
    ppermute x3, waiting for transfers between devices: 3.41 us -> 9.92 us  [shifted(): return lax.ppermute(block, axis, route)]
  transfers between devices with their start and end apart: 17 -> 15, of which waited for: 13 -> 14; matrix products, arithmetic and copies ran while one was open for 12% -> 8% of each run, Pallas kernels for 0% -> 0%
where the time goes in v1:
time: 580 us; the launch traced here: 578 us
  blocking collectives  235 us (41%)
  waiting for transfers between devices  154 us (27%)
  starting transfers between devices  58 us (10%)
  matrix products  57.8 us (10%)
  local copies, waits for them, and re-layouts  41.9 us (7%)
  between operations  15.7 us (3%)
  other arithmetic  15.3 us (3%)
    all_gather x1, blocking collectives, gather_in_order(): tiles = lax.all_gather(tiles, axes[k])  187 us
    all_to_all x2, waiting for transfers between devices, sum_at_owner(): lax.all_to_all(tiles, axis, split_axis=0, concat_axis=0, tiled=True)  98.9 us
    all_to_all x2, blocking collectives, copy_for_each(): lax.all_to_all(jnp.broadcast_to(array[None], (devices, *array.shape)), ax...  48.1 us
    dot_general x54, matrix products, causal_taps(): jnp.dot(window.reshape(-1, channels_in), kernel, preferred_element_type=j...  37.6 us
    all_to_all x3, waiting for transfers between devices, copy_for_each(): lax.all_to_all(jnp.broadcast_to(array[None], (devices, *array.shape)), ax...  24 us
    all_to_all x3, starting transfers between devices, copy_for_each(): lax.all_to_all(jnp.broadcast_to(array[None], (devices, *array.shape)), ax...  22.2 us
    dot_general x27, matrix products, transposed_taps(): lax.dot_general(window.reshape(-1, channels_out), kernel, (((1,), (1,)),...  14.1 us
  transfers between devices with their start and end apart: 15, of which 14 were waited for; matrix products, arithmetic and copies ran while one was open for 8% of the time, Pallas kernels for 0%

profile of v1, /device:TPU:2, one launch (start us, length us, event | category | flops | bytes accessed | tf_op | source)
XLA Modules:
  0.0 577.9 jit_solution(16864679262984026640)
XLA Ops:
  8.5 22.7 %all_to_all.58 = f32[8,1,16]{2,1,0:T(1,128)S(1)} all-to-all(f32[8,1,16]{2,1,0:T(1,128)S(1)} %broadcast_in_dim.10), channel_id=1, replica_groups=mesh['dp'=16,'tm'=8,'height'=4] {'tm'}, dimensions={0} | all-to-all | bytes 1024 | tf_op jit(solution)/shard_map/all_to_all | solution.py:13
  32.6 2.5 collective-permute-start
  35.1 1.9 collective-permute-done
  37.9 4.5 all-to-all-start.1
  42.3 1.3 copy.74
  43.7 6.8 %all-to-all-done.1 = bf16[4,4,8,16,128]{4,3,2,1,0:T(8,128)(2,1)S(1)} async-done(((bf16[4,4,8,16,128]{4,3,2,1,0:T(8,128)(2,1)}), bf16[4,4,8,16,128]{4,3,2,1,0:T(8,128)(2,1)S(1)}, u32[]{:S(2)}, u32[]{:S(2)}) %all-to-all-start.1) | async-done | bytes 524320 | tf_op jit(solution)/shard_map/all_to_all | solution.py:13
  51.5 25.4 %all_to_all.59 = bf16[4,128,2048]{1,2,0:T(8,128)(2,1)S(1)} all-to-all(bf16[4,128,2048]{1,2,0:T(8,128)(2,1)S(1)} %broadcast_in_dim.12), channel_id=1, replica_groups=mesh['dp'=16,'tm'=8,'height'=4] {'height'}, dimensions={0} | all-to-all | bytes 4194304 | tf_op jit(solution)/shard_map/all_to_all | solution.py:13
  76.9 2.2 stack.2
  79.1 4.7 all-to-all-start.2
  83.8 187.2 %all-gather = bf16[1728,256]{1,0:T(8,128)(2,1)} all-gather(bf16[216,256]{1,0:T(8,128)(2,1)S(1)} %copy-done.59), channel_id=2, replica_groups=mesh['dp'=16,'tm'=8,'height'=4] {'tm'}, dimensions={0}, use_global_device_ids=true | all-gather | bytes 995328 | tf_op jit(solution)/shard_map/all_gather | solution.py:68
  271.0 1.3 collective-permute-start.4
  272.4 5.5 collective-permute-done.4
  277.9 1.3 collective-permute-start.6
  279.2 4.7 collective-permute-start.5
  284.5 3.3 collective-permute-done.5
  288.2 1.4 pad_maximum_fusion.1
  289.6 2.3 fusion.149
  294.9 1.2 pad_slice_fusion.1
  296.0 2.3 pad_slice_fusion
  298.4 2.7 copy.75
  301.0 4.0 copy.76
  305.0 11.6 %all-gather.4.cloned.1.call-done = bf16[32,216,256]{2,1,0:T(8,128)(2,1)} async-done(((bf16[8,216,256]{2,1,0:T(8,128)(2,1)}), bf16[32,216,256]{2,1,0:T(8,128)(2,1)}) %all-gather.4.cloned.1.call-update) | async-done | bytes 3538960 | tf_op jit(solution)/shard_map/all_gather | solution.py:68
  316.6 2.4 copy.79
  326.7 1.3 fusion.72
  328.0 1.2 convolution_add_fusion.72
  329.3 1.2 convolution_add_fusion.71
  330.5 1.2 convolution_add_fusion.70
  331.8 1.2 convolution_add_fusion.69
  333.0 1.2 convolution_add_fusion.68
  335.5 1.2 convolution_add_fusion.66
  336.7 1.2 convolution_add_fusion.65
  337.9 1.2 convolution_add_fusion.64
  340.2 1.2 convolution_add_fusion.62
  341.4 1.2 convolution_add_fusion.61
  342.6 1.2 convolution_add_fusion.60
  345.0 1.2 convolution_add_fusion.58
  359.3 3.9 all-to-all-start.3
  363.2 2.2 convolution_add_fusion.1
  365.4 3.5 all-to-all-done.3
  368.9 1.5 copy.119
  370.4 1.5 reshape.494
  371.9 3.7 fusion.146
  379.8 11.2 %all-to-all-start.5 = ((f32[32,1,64]{2,1,0:T(1,128)}), f32[32,1,64]{2,1,0:T(1,128)S(1)}, u32[]{:S(2)}, u32[]{:S(2)}) async-start(f32[32,1,64]{2,1,0:T(1,128)} %broadcast_in_dim.13), calls=%async_computation.5 | async-start | bytes 32768 | tf_op jit(solution)/shard_map/all_to_all | solution.py:13
  391.0 2.0 fusion.74
  393.1 2.3 copy.77
  395.3 2.2 reshape.491
  397.5 5.8 %all-to-all-done.5 = f32[32,1,64]{2,1,0:T(1,128)S(1)} async-done(((f32[32,1,64]{2,1,0:T(1,128)}), f32[32,1,64]{2,1,0:T(1,128)S(1)}, u32[]{:S(2)}, u32[]{:S(2)}) %all-to-all-start.5) | async-done | bytes 8224 | tf_op jit(solution)/shard_map/all_to_all | solution.py:13
  403.8 1.2 slice_multiply_fusion
  407.2 2.8 fusion.145
  410.7 6.6 %all-to-all-start.6 = ((f32[32,1,512]{2,1,0:T(1,128)}), f32[32,1,512]{2,1,0:T(1,128)S(1)}, u32[]{:S(2)}, u32[]{:S(2)}) async-start(f32[32,1,512]{2,1,0:T(1,128)} %broadcast_in_dim.14), calls=%async_computation.6 | async-start | bytes 131072 | tf_op jit(solution)/shard_map/all_to_all | solution.py:13
  417.2 1.4 reshape.490
  418.7 11.5 %all-to-all-done.6 = f32[32,1,512]{2,1,0:T(1,128)S(1)} async-done(((f32[32,1,512]{2,1,0:T(1,128)}), f32[32,1,512]{2,1,0:T(1,128)S(1)}, u32[]{:S(2)}, u32[]{:S(2)}) %all-to-all-start.6) | async-done | bytes 65568 | tf_op jit(solution)/shard_map/all_to_all | solution.py:13
  431.6 2.2 add_convert_fusion
  433.8 2.3 collective-permute-start.1
  436.1 2.5 collective-permute-done.1
  438.6 1.3 collective-permute-start.3
  439.9 4.6 collective-permute-start.2
  445.1 1.5 collective-permute-done.2
  449.6 1.4 copy-done.9
  451.0 5.2 all-to-all-start.7
  458.0 1.3 copy-done.1
  465.9 92.8 %all-to-all-done.7 = f32[8,288,256]{2,1,0:T(8,128)S(1)} async-done(((f32[8,288,256]{2,1,0:T(8,128)}), f32[8,288,256]{2,1,0:T(8,128)S(1)}, u32[]{:S(2)}, u32[]{:S(2)}) %all-to-all-start.7) | async-done | bytes 2359328 | tf_op jit(solution)/shard_map/all_to_all | solution.py:86
  559.5 4.0 all-to-all-start.8
  564.3 6.1 %all-to-all-done.8 = f32[4,72,256]{2,1,0:T(8,128)S(1)} async-done(((f32[4,72,256]{2,1,0:T(8,128)}), f32[4,72,256]{2,1,0:T(8,128)S(1)}, u32[]{:S(2)}, u32[]{:S(2)}) %all-to-all-start.8) | async-done | bytes 294944 | tf_op jit(solution)/shard_map/all_to_all | solution.py:86
  (269 shorter events, 55.2 us)
Async XLA Ops:
  32.6 4.4 collective-permute-start
  37.9 12.5 %all-to-all-start.1 = ((bf16[4,4,8,16,128]{4,3,2,1,0:T(8,128)(2,1)}), bf16[4,4,8,16,128]{4,3,2,1,0:T(8,128)(2,1)S(1)}, u32[]{:S(2)}, u32[]{:S(2)}) async-start(bf16[4,4,8,16,128]{4,3,2,1,0:T(8,128)(2,1)} %broadcast_in_dim.11), calls=%async_computation.1 | async-start | bytes 1048576 | tf_op jit(solution)/shard_map/all_to_all | solution.py:13
  43.6 33.2 %copy-start.56 = (bf16[1728,128]{1,0:T(8,128)(2,1)S(1)}, bf16[1728,128]{1,0:T(8,128)(2,1)}, u32[]{:S(2)}) copy-start(bf16[1728,128]{1,0:T(8,128)(2,1)} %param.12) | copy-start | bytes 1327108
  79.1 4.7 copy-start.59
  79.1 191.9 %copy-start.6 = (bf16[4,4,32,256]{3,2,1,0:T(8,128)(2,1)S(1)}, bf16[4,4,32,256]{3,2,1,0:T(8,128)(2,1)}, u32[]{:S(2)}) copy-start(bf16[4,4,32,256]{3,2,1,0:T(8,128)(2,1)} %param.17) | copy-start | bytes 786436
  79.1 247.6 %all-to-all-start.2 = ((bf16[8,1728,128]{2,1,0:T(8,128)(2,1)}), bf16[8,1728,128]{2,1,0:T(8,128)(2,1)}, u32[]{:S(2)}, u32[]{:S(2)}) async-start(bf16[8,1728,128]{2,1,0:T(8,128)(2,1)} %stack.2), calls=%async_computation.2 | async-start | bytes 7077888 | tf_op jit(solution)/shard_map/all_to_all | solution.py:187
  83.8 232.8 %all-gather.4.cloned.1.call-start = ((), (), s32[]{:S(2)}) async-start(), calls=%async_computation.9 | async-start | bytes 4423680 | tf_op jit(solution)/shard_map/all_gather | solution.py:68
  271.0 6.9 %collective-permute-start.4 = (bf16[2,4,32,256]{3,2,1,0:T(8,128)(2,1)S(1)}, bf16[2,4,32,256]{3,2,1,0:T(8,128)(2,1)S(1)}, u32[]{:S(2)}, u32[]{:S(2)}) collective-permute-start(bf16[2,4,32,256]{3,2,1,0:T(8,128)(2,1)S(1)} %slice.629), channel_id=1, source_target_pairs={{4,0},{8,4},{12,8},{16,12},{20,16},{24,20},{28,24},{5,1},{9,5},{13... | collective-permute-start | bytes 393224 | tf_op jit(solution)/shard_map/ppermute | solution.py:34
  277.9 6.5 %collective-permute-start.6 = (bf16[6,1,32,256]{3,2,1,0:T(8,128)(2,1)S(1)}, bf16[6,1,32,256]{3,2,1,0:T(8,128)(2,1)S(1)}, u32[]{:S(2)}, u32[]{:S(2)}) collective-permute-start(bf16[6,1,32,256]{3,2,1,0:T(8,128)(2,1)S(1)} %get-tuple-element.98), channel_id=1, source_target_pairs={{1,0},{2,1},{3,2},{5,4},{6,5},{7,6},{9,8},{10,9},{11,10},{13,12},{... | collective-permute-start | bytes 294920 | tf_op jit(solution)/shard_map/ppermute | solution.py:58
  279.2 8.6 %collective-permute-start.5 = (bf16[6,1,32,256]{3,2,1,0:T(8,128)(2,1)S(1)}, bf16[6,1,32,256]{3,2,1,0:T(8,128)(2,1)S(1)}, u32[]{:S(2)}, u32[]{:S(2)}) collective-permute-start(bf16[6,1,32,256]{3,2,1,0:T(8,128)(2,1)S(1)} %get-tuple-element.97), channel_id=1, source_target_pairs={{0,1},{1,2},{2,3},{4,5},{5,6},{6,7},{8,9},{9,10},{10,11},{12,13},{... | collective-permute-start | bytes 294920 | tf_op jit(solution)/shard_map/ppermute | solution.py:56
  289.6 2.3 copy-start.3
  316.6 2.4 copy-start.16
  316.6 2.7 copy-start.15
  316.6 3.0 copy-start.14
  316.6 3.3 copy-start.13
  319.0 88.2 %copy-start = (bf16[8,4,216,256]{3,2,1,0:T(8,128)(2,1)}, bf16[8,4,216,256]{3,2,1,0:T(8,128)(2,1)S(1)}, u32[]{:S(2)}) copy-start(bf16[8,4,216,256]{3,2,1,0:T(8,128)(2,1)S(1)} %copy.79) | copy-start | bytes 10616836
  319.0 1.7 copy-start.37
  319.3 1.7 copy-start.12
  319.9 1.4 copy-start.36
  320.2 1.4 copy-start.30
  320.5 1.4 copy-start.35
  320.7 1.4 copy-start.33
  322.5 1.4 copy-start.23
  322.8 1.4 copy-start.28
  323.0 1.4 copy-start.27
  326.7 7.6 %copy-start.53 = (bf16[2,8,16,512]{3,2,1,0:T(8,128)(2,1)S(1)}, bf16[2,8,16,512]{3,2,1,0:T(8,128)(2,1)}, u32[]{:S(2)}) copy-start(bf16[2,8,16,512]{3,2,1,0:T(8,128)(2,1)} %get-tuple-element.58) | copy-start | bytes 786436
  326.7 8.8 %copy-start.52 = (bf16[2,8,16,512]{3,2,1,0:T(8,128)(2,1)S(1)}, bf16[2,8,16,512]{3,2,1,0:T(8,128)(2,1)}, u32[]{:S(2)}) copy-start(bf16[2,8,16,512]{3,2,1,0:T(8,128)(2,1)} %get-tuple-element.59) | copy-start | bytes 786436
  326.7 10.0 %copy-start.51 = (bf16[2,8,16,512]{3,2,1,0:T(8,128)(2,1)S(1)}, bf16[2,8,16,512]{3,2,1,0:T(8,128)(2,1)}, u32[]{:S(2)}) copy-start(bf16[2,8,16,512]{3,2,1,0:T(8,128)(2,1)} %get-tuple-element.60) | copy-start | bytes 786436
  326.7 11.2 %copy-start.50 = (bf16[2,8,16,512]{3,2,1,0:T(8,128)(2,1)S(1)}, bf16[2,8,16,512]{3,2,1,0:T(8,128)(2,1)}, u32[]{:S(2)}) copy-start(bf16[2,8,16,512]{3,2,1,0:T(8,128)(2,1)} %get-tuple-element.61) | copy-start | bytes 786436
  326.7 12.4 %copy-start.49 = (bf16[2,8,16,512]{3,2,1,0:T(8,128)(2,1)S(1)}, bf16[2,8,16,512]{3,2,1,0:T(8,128)(2,1)}, u32[]{:S(2)}) copy-start(bf16[2,8,16,512]{3,2,1,0:T(8,128)(2,1)} %get-tuple-element.62) | copy-start | bytes 786436
  326.7 13.5 %copy-start.48 = (bf16[2,8,16,512]{3,2,1,0:T(8,128)(2,1)S(1)}, bf16[2,8,16,512]{3,2,1,0:T(8,128)(2,1)}, u32[]{:S(2)}) copy-start(bf16[2,8,16,512]{3,2,1,0:T(8,128)(2,1)} %get-tuple-element.63) | copy-start | bytes 786436
  328.0 13.4 %copy-start.47 = (bf16[2,8,16,512]{3,2,1,0:T(8,128)(2,1)S(1)}, bf16[2,8,16,512]{3,2,1,0:T(8,128)(2,1)}, u32[]{:S(2)}) copy-start(bf16[2,8,16,512]{3,2,1,0:T(8,128)(2,1)} %get-tuple-element.64) | copy-start | bytes 786436
  329.3 13.3 %copy-start.22 = (bf16[2,8,16,4,128]{4,3,2,1,0:T(4,128)(2,1)S(1)}, bf16[2,8,16,4,128]{4,3,2,1,0:T(4,128)(2,1)}, u32[]{:S(2)}) copy-start(bf16[2,8,16,4,128]{4,3,2,1,0:T(4,128)(2,1)} %copy.70) | copy-start | bytes 786436
  330.5 13.3 %copy-start.46 = (bf16[2,8,16,512]{3,2,1,0:T(8,128)(2,1)S(1)}, bf16[2,8,16,512]{3,2,1,0:T(8,128)(2,1)}, u32[]{:S(2)}) copy-start(bf16[2,8,16,512]{3,2,1,0:T(8,128)(2,1)} %get-tuple-element.65) | copy-start | bytes 786436
  331.8 13.2 %copy-start.45 = (bf16[2,8,16,512]{3,2,1,0:T(8,128)(2,1)S(1)}, bf16[2,8,16,512]{3,2,1,0:T(8,128)(2,1)}, u32[]{:S(2)}) copy-start(bf16[2,8,16,512]{3,2,1,0:T(8,128)(2,1)} %get-tuple-element.66) | copy-start | bytes 786436
  333.0 13.1 %copy-start.44 = (bf16[2,8,16,512]{3,2,1,0:T(8,128)(2,1)S(1)}, bf16[2,8,16,512]{3,2,1,0:T(8,128)(2,1)}, u32[]{:S(2)}) copy-start(bf16[2,8,16,512]{3,2,1,0:T(8,128)(2,1)} %get-tuple-element.67) | copy-start | bytes 786436
  334.3 13.0 %copy-start.43 = (bf16[2,8,16,512]{3,2,1,0:T(8,128)(2,1)S(1)}, bf16[2,8,16,512]{3,2,1,0:T(8,128)(2,1)}, u32[]{:S(2)}) copy-start(bf16[2,8,16,512]{3,2,1,0:T(8,128)(2,1)} %get-tuple-element.68) | copy-start | bytes 786436
  335.5 13.0 %copy-start.42 = (bf16[2,8,16,512]{3,2,1,0:T(8,128)(2,1)S(1)}, bf16[2,8,16,512]{3,2,1,0:T(8,128)(2,1)}, u32[]{:S(2)}) copy-start(bf16[2,8,16,512]{3,2,1,0:T(8,128)(2,1)} %get-tuple-element.69) | copy-start | bytes 786436
  336.7 12.9 %copy-start.41 = (bf16[2,8,16,512]{3,2,1,0:T(8,128)(2,1)S(1)}, bf16[2,8,16,512]{3,2,1,0:T(8,128)(2,1)}, u32[]{:S(2)}) copy-start(bf16[2,8,16,512]{3,2,1,0:T(8,128)(2,1)} %get-tuple-element.70) | copy-start | bytes 786436
  337.9 12.9 %copy-start.40 = (bf16[2,8,16,512]{3,2,1,0:T(8,128)(2,1)S(1)}, bf16[2,8,16,512]{3,2,1,0:T(8,128)(2,1)}, u32[]{:S(2)}) copy-start(bf16[2,8,16,512]{3,2,1,0:T(8,128)(2,1)} %get-tuple-element.71) | copy-start | bytes 786436
  339.0 12.8 %copy-start.20 = (bf16[2,8,16,512]{3,2,1,0:T(8,128)(2,1)S(1)}, bf16[2,8,16,512]{3,2,1,0:T(8,128)(2,1)}, u32[]{:S(2)}) copy-start(bf16[2,8,16,512]{3,2,1,0:T(8,128)(2,1)} %get-tuple-element.73) | copy-start | bytes 786436
  340.2 12.8 %copy-start.21 = (bf16[2,8,16,4,128]{4,3,2,1,0:T(4,128)(2,1)S(1)}, bf16[2,8,16,4,128]{4,3,2,1,0:T(4,128)(2,1)}, u32[]{:S(2)}) copy-start(bf16[2,8,16,4,128]{4,3,2,1,0:T(4,128)(2,1)} %copy.71) | copy-start | bytes 786436
  341.4 12.7 %copy-start.19 = (bf16[2,8,16,512]{3,2,1,0:T(8,128)(2,1)S(1)}, bf16[2,8,16,512]{3,2,1,0:T(8,128)(2,1)}, u32[]{:S(2)}) copy-start(bf16[2,8,16,512]{3,2,1,0:T(8,128)(2,1)} %get-tuple-element.74) | copy-start | bytes 786436
  342.6 12.7 %copy-start.18 = (bf16[2,8,16,512]{3,2,1,0:T(8,128)(2,1)S(1)}, bf16[2,8,16,512]{3,2,1,0:T(8,128)(2,1)}, u32[]{:S(2)}) copy-start(bf16[2,8,16,512]{3,2,1,0:T(8,128)(2,1)} %get-tuple-element.75) | copy-start | bytes 786436
  343.8 12.6 %copy-start.17 = (bf16[2,8,16,512]{3,2,1,0:T(8,128)(2,1)S(1)}, bf16[2,8,16,512]{3,2,1,0:T(8,128)(2,1)}, u32[]{:S(2)}) copy-start(bf16[2,8,16,512]{3,2,1,0:T(8,128)(2,1)} %get-tuple-element.72) | copy-start | bytes 786436
  345.0 12.6 %copy-start.39 = (bf16[2,8,16,512]{3,2,1,0:T(8,128)(2,1)S(1)}, bf16[2,8,16,512]{3,2,1,0:T(8,128)(2,1)}, u32[]{:S(2)}) copy-start(bf16[2,8,16,512]{3,2,1,0:T(8,128)(2,1)} %get-tuple-element.53) | copy-start | bytes 786436
  346.2 12.5 %copy-start.54 = (bf16[2,8,16,128]{3,2,1,0:T(8,128)(2,1)S(1)}, bf16[2,8,16,128]{3,2,1,0:T(8,128)(2,1)}, u32[]{:S(2)}) copy-start(bf16[2,8,16,128]{3,2,1,0:T(8,128)(2,1)} %param.9) | copy-start | bytes 196612
  359.3 9.6 %all-to-all-start.3 = ((bf16[2,8,16,128]{3,2,0,1:T(8,128)(2,1)}), bf16[2,8,16,128]{3,2,0,1:T(8,128)(2,1)}, u32[]{:S(2)}, u32[]{:S(2)}) async-start(bf16[2,8,16,128]{3,2,0,1:T(8,128)(2,1)} %fusion.45), calls=%async_computation.3 | async-start | bytes 131072 | tf_op jit(solution)/shard_map/all_to_all | solution.py:193
  379.8 23.5 %all-to-all-start.5 = ((f32[32,1,64]{2,1,0:T(1,128)}), f32[32,1,64]{2,1,0:T(1,128)S(1)}, u32[]{:S(2)}, u32[]{:S(2)}) async-start(f32[32,1,64]{2,1,0:T(1,128)} %broadcast_in_dim.13), calls=%async_computation.5 | async-start | bytes 32768 | tf_op jit(solution)/shard_map/all_to_all | solution.py:13
  407.2 23.0 %copy-start.60 = (f32[256]{0:T(256)S(1)}, f32[256]{0:T(256)}, u32[]{:S(2)}) copy-start(f32[256]{0:T(256)} %param.14) | copy-start | bytes 3076
  407.2 24.3 %copy-start.61 = (f32[256]{0:T(256)S(1)}, f32[256]{0:T(256)}, u32[]{:S(2)}) copy-start(f32[256]{0:T(256)} %mul.160) | copy-start | bytes 3076
  407.2 24.3 %copy-start.62 = (f32[256]{0:T(256)S(1)}, f32[256]{0:T(256)}, u32[]{:S(2)}) copy-start(f32[256]{0:T(256)} %sub.74) | copy-start | bytes 3076
  407.2 24.3 %copy-start.63 = (f32[256]{0:T(256)S(1)}, f32[256]{0:T(256)}, u32[]{:S(2)}) copy-start(f32[256]{0:T(256)} %param.15) | copy-start | bytes 3076
  410.0 37.0 %copy-start.8 = (bf16[4,4,32,256]{3,2,1,0:T(8,128)(2,1)S(1)}, bf16[4,4,32,256]{3,2,1,0:T(8,128)(2,1)}, u32[]{:S(2)}) copy-start(bf16[4,4,32,256]{3,2,1,0:T(8,128)(2,1)} %param.17) | copy-start | bytes 786436
  410.7 19.4 %all-to-all-start.6 = ((f32[32,1,512]{2,1,0:T(1,128)}), f32[32,1,512]{2,1,0:T(1,128)S(1)}, u32[]{:S(2)}, u32[]{:S(2)}) async-start(f32[32,1,512]{2,1,0:T(1,128)} %broadcast_in_dim.14), calls=%async_computation.6 | async-start | bytes 131072 | tf_op jit(solution)/shard_map/all_to_all | solution.py:13
  418.6 26.5 %copy-start.4 = (f32[4,4,32,256]{3,2,1,0:T(8,128)}, f32[4,4,32,256]{3,2,1,0:T(8,128)S(1)}, u32[]{:S(2)}) copy-start(f32[4,4,32,256]{3,2,1,0:T(8,128)S(1)} %reshape.490) | copy-start | bytes 1572868
  433.8 4.8 collective-permute-start.1
  438.6 6.5 %collective-permute-start.3 = (bf16[6,1,32,256]{3,2,1,0:T(8,128)(2,1)S(1)}, bf16[6,1,32,256]{3,2,1,0:T(8,128)(2,1)S(1)}, u32[]{:S(2)}, u32[]{:S(2)}) collective-permute-start(bf16[6,1,32,256]{3,2,1,0:T(8,128)(2,1)S(1)} %get-tuple-element.104), channel_id=1, source_target_pairs={{1,0},{2,1},{3,2},{5,4},{6,5},{7,6},{9,8},{10,9},{11,10},{13,12},{... | collective-permute-start | bytes 294920 | tf_op jit(solution)/shard_map/ppermute | solution.py:58
  439.9 6.8 %collective-permute-start.2 = (bf16[6,1,32,256]{3,2,1,0:T(8,128)(2,1)S(1)}, bf16[6,1,32,256]{3,2,1,0:T(8,128)(2,1)S(1)}, u32[]{:S(2)}, u32[]{:S(2)}) collective-permute-start(bf16[6,1,32,256]{3,2,1,0:T(8,128)(2,1)S(1)} %get-tuple-element.103), channel_id=1, source_target_pairs={{0,1},{1,2},{2,3},{4,5},{5,6},{6,7},{8,9},{9,10},{10,11},{12,13},{... | collective-permute-start | bytes 294920 | tf_op jit(solution)/shard_map/ppermute | solution.py:56
  445.1 3.9 copy-start.57
  451.0 107.7 %all-to-all-start.7 = ((f32[8,288,256]{2,1,0:T(8,128)}), f32[8,288,256]{2,1,0:T(8,128)S(1)}, u32[]{:S(2)}, u32[]{:S(2)}) async-start(f32[8,288,256]{2,1,0:T(8,128)} %bitcast.330), calls=%async_computation.7 | async-start | bytes 4718592 | tf_op jit(solution)/shard_map/all_to_all | solution.py:86
  457.3 2.0 copy-start.1
  465.2 98.3 %copy-start.5 = (f32[4,4,32,256]{3,2,1,0:T(8,128)S(1)}, f32[4,4,32,256]{3,2,1,0:T(8,128)}, u32[]{:S(2)}) copy-start(f32[4,4,32,256]{3,2,1,0:T(8,128)} %copy-done.4) | copy-start | bytes 1572868
  559.5 10.8 %all-to-all-start.8 = ((f32[4,72,256]{2,1,0:T(8,128)}), f32[4,72,256]{2,1,0:T(8,128)S(1)}, u32[]{:S(2)}, u32[]{:S(2)}) async-start(f32[4,72,256]{2,1,0:T(8,128)} %bitcast.333), calls=%async_computation.8 | async-start | bytes 589824 | tf_op jit(solution)/shard_map/all_to_all | solution.py:86
  (15 other events, 19.9 us)
Sparse Core Ops, SparseCore 0:
  271.1 45.4 all-gather.3
